TPU v7x, 32 devices: a whole 2x2x4 slice. The times are simulated.
32 devices in a mesh: sec: 4 (over y, core), op: 8 (over z, x).
Axes of the slice: x: 2, y: 2, z: 4, core: 2. Of those that a mesh axis runs over, the one named last changes fastest.
Arguments:
- wavefunction: bfloat16 [8, 256, 256], P('sec'), may hold values from -6 to 6
- diagonal: bfloat16 [8, 256, 256], P('sec'), may hold values from 1 to 4
- preconditioner: bfloat16 [8, 256, 256], P('sec'), may hold values from 0.25 to 1
- left_operator_blocks: bfloat16 [512, 256, 256], P(('sec', 'op')), may hold values from -0.1875 to 0.1875
- right_operator_blocks: bfloat16 [512, 256, 256], P(('sec', 'op')), may hold values from -0.375 to 0.375
- slot_source_sector: int32 [512], P(('sec', 'op')), may hold values from 0 to 7
- slot_target_sector: int32 [512], P(('sec', 'op')), may hold values from 0 to 1
- pair_count: int32 [32], P(('sec', 'op')), may hold values from 1 to 16, as said below
- left_dims: int32 [8], replicated, may hold values from 128 to 256, as said below
- right_dims: int32 [8], replicated, may hold values from 128 to 256, as said below
Outputs:
- correction: bfloat16 [8, 256, 256], P('sec')
- product_rows: float32 [8, 256, 256], P('sec', 'op')
- projected: float32 [3], replicated
Inputs may be any that keep to these rules, and one draw needn't show every extreme that they name: `pair_count`: slots below a device's count hold pairs, the rest are ignored; some device has all 16 slots live. `left_dims`: some sector uses all 256 rows. `right_dims`: some sector uses all 256 columns.
All inputs are finite; a program needn't handle non-finite values.
Results may differ from a plain program's by a relative error of at most 0.003.
Values may be sent and summed in bfloat16 or wider, within the bound.
A program may use at most 64 MiB of HBM per device.

v0:
```python
import jax
import jax.numpy as jnp
from jax import lax
from jax.sharding import PartitionSpec as P


def block_mask(left_dims, right_dims, block_size):
    positions = jnp.arange(block_size, dtype=jnp.int32)
    return (positions[None, :, None] < left_dims[:, None, None]) & (
        positions[None, None, :] < right_dims[:, None, None]
    )


def gather_sources(own_vector):
    return lax.all_gather(own_vector, "sec", axis=0, tiled=True)


def reduce_dots(values):
    return lax.psum(values, "sec")


def pair_partial(
    sources,
    left_operator_blocks,
    right_operator_blocks,
    slot_source_sector,
    slot_target_sector,
    live_count,
    sector_count,
):
    block_size = sources.shape[1]
    zero_sum = jnp.zeros((sector_count, block_size, block_size), jnp.float32)

    def add_pair(slot_index, partial_value):
        source_block = lax.dynamic_index_in_dim(
            sources, slot_source_sector[slot_index], 0, keepdims=False
        )
        middle = jnp.dot(
            left_operator_blocks[slot_index], source_block, preferred_element_type=jnp.float32
        )
        contribution = jnp.dot(
            middle,
            right_operator_blocks[slot_index].astype(jnp.float32),
            precision=lax.Precision.HIGHEST,
            preferred_element_type=jnp.float32,
        )
        contribution = jnp.where(slot_index < live_count, contribution, 0.0)
        return partial_value.at[slot_target_sector[slot_index]].add(contribution)

    return lax.fori_loop(0, left_operator_blocks.shape[0], add_pair, zero_sum)


def sum_pairs(partial_value):
    return lax.psum(partial_value, "op")


def on_device(
    wavefunction,
    diagonal,
    preconditioner,
    left_operator_blocks,
    right_operator_blocks,
    slot_source_sector,
    slot_target_sector,
    pair_count,
    left_dims,
    right_dims,
):
    sector_count = wavefunction.shape[0]
    block_size = wavefunction.shape[1]
    op_devices = lax.axis_size("op")
    share_rows = block_size // op_devices
    first_sector = lax.axis_index("sec") * sector_count
    row_start = lax.axis_index("op") * share_rows
    entries = float(left_dims.shape[0] * block_size * block_size)
    own_mask = block_mask(
        lax.dynamic_slice_in_dim(left_dims, first_sector, sector_count),
        lax.dynamic_slice_in_dim(right_dims, first_sector, sector_count),
        block_size,
    )
    live_count = pair_count[0]
    own_vector = jnp.where(own_mask, wavefunction, jnp.zeros_like(wavefunction))
    diag_view = diagonal.astype(jnp.float32)
    scale_view = preconditioner.astype(jnp.float32)
    vector_view = own_vector.astype(jnp.float32)

    def apply_operator(sources, field_view):
        partial_value = pair_partial(
            sources,
            left_operator_blocks,
            right_operator_blocks,
            slot_source_sector,
            slot_target_sector,
            live_count,
            sector_count,
        )
        return jnp.where(own_mask, diag_view * field_view + sum_pairs(partial_value), 0.0)

    sigma_first = apply_operator(gather_sources(own_vector), vector_view)
    norm_vector, correlation = reduce_dots(
        (jnp.sum(vector_view * vector_view), jnp.sum(vector_view * sigma_first))
    )
    rayleigh = correlation / norm_vector
    residual = sigma_first - rayleigh * vector_view
    scaled = scale_view * residual
    along_vector = reduce_dots((jnp.sum(vector_view * scaled),))[0]
    orthogonal = scaled - along_vector / norm_vector * vector_view
    square_norm = reduce_dots((jnp.sum(orthogonal * orthogonal),))[0]
    corr_view = (orthogonal * lax.rsqrt(square_norm / entries + 1e-06)).astype(jnp.bfloat16)
    next_sources = gather_sources(corr_view)
    corr_float = corr_view.astype(jnp.float32)
    sigma_second = apply_operator(next_sources, corr_float)
    cross_term, self_term = reduce_dots(
        (jnp.sum(vector_view * sigma_second), jnp.sum(corr_float * sigma_second))
    )
    projected = jnp.stack(
        [rayleigh, cross_term * lax.rsqrt(norm_vector * entries), self_term / entries]
    )
    product_rows = lax.dynamic_slice_in_dim(sigma_second, row_start, share_rows, 1)
    return (corr_view, product_rows, projected)


def solution(mesh):
    in_specs = (
        P("sec", None, None),
        P("sec", None, None),
        P("sec", None, None),
        P(("sec", "op"), None, None),
        P(("sec", "op"), None, None),
        P(("sec", "op")),
        P(("sec", "op")),
        P(("sec", "op")),
        P(),
        P(),
    )
    out_specs = (P("sec", None, None), P("sec", "op", None), P())
    return jax.shard_map(
        on_device, mesh=mesh, in_specs=in_specs, out_specs=out_specs, check_vma=False
    )
```

profile of v0, /device:TPU:0, one launch (start us, length us, event | category | flops | bytes accessed | tf_op | source)
XLA Modules:
  0.0 568.9 jit_solution(6976858668424904572)
XLA Ops:
  10.6 19.5 %all-gather.3.cloned.1.call-done = bf16[8,256,256]{2,1,0:T(8,128)(2,1)} async-done(((bf16[2,256,256]{2,1,0:T(8,128)(2,1)}), bf16[8,256,256]{2,1,0:T(8,128)(2,1)}) %all-gather.3.cloned.1.call-update) | async-done | bytes 1048592 | tf_op jit(solution)/shard_map/all_gather | solution.py:15
  30.2 182.8 %while.28 = (s32[]{:T(128)}, f32[2,256,256]{2,1,0:T(8,128)S(1)}, s32[16]{0:T(128)}, s32[]{:T(128)}, bf16[16,256,256]{2,1,0:T(8,128)(2,1)}, /*index=5*/s32[16]{0:...) while((s32[]{:T(128)}, f32[2,256,256]{2,1,0:T(8,128)S(1)}, ...), condition=%wide.region_2.3_spmd, body=%wide.region_0.2_spmd.sunk | while | flops 235077664 | bytes 1444100 | solution.py:50
  39.9 1.8 fusion.55
  51.3 1.8 fusion.55
  62.7 1.8 fusion.55
  74.1 1.8 fusion.55
  85.5 1.8 fusion.55
  108.4 1.8 fusion.55
  131.2 1.8 fusion.55
  154.1 1.8 fusion.55
  165.5 1.8 fusion.55
  176.9 1.8 fusion.55
  199.7 1.8 fusion.55
  213.9 72.5 %all-reduce.5.cloned.1.call-done = f32[2,256,256]{2,1,0:T(8,128)} async-done(((f32[2,256,256]{2,1,0:T(8,128)}), f32[2,256,256]{2,1,0:T(8,128)}) %all-reduce.5.cloned.1.call-update) | async-done | bytes 524304 | tf_op jit(solution)/shard_map/psum | solution.py:54
  286.4 2.0 fusion.30
  288.4 6.3 %all-reduce.1 = (f32[]{:T(128)}, f32[]{:T(128)}) all-reduce(f32[]{:T(128)} %get-tuple-element.330, f32[]{:T(128)} %get-tuple-element.329), channel_id=1, replica_groups=mesh['sec'=4,'op'=8] {'sec'}, use_global_device_ids=true, to_apply=%region_5.6 | all-reduce | flops 2 | bytes 16 | tf_op jit(solution)/shard_map/psum | solution.py:19
  296.1 2.0 fusion.33
  298.1 7.2 %psum.59 = f32[]{:T(128)} all-reduce(f32[]{:T(128)} %fusion.33), channel_id=1, replica_groups=mesh['sec'=4,'op'=8] {'sec'}, use_global_device_ids=true, to_apply=%region_9.10 | all-reduce | flops 1 | bytes 8 | tf_op jit(solution)/shard_map/psum | solution.py:19
  307.7 6.5 %psum.60 = f32[]{:T(128)} all-reduce(f32[]{:T(128)} %multiply_reduce_fusion), channel_id=1, replica_groups=mesh['sec'=4,'op'=8] {'sec'}, use_global_device_ids=true, to_apply=%region_11.12 | all-reduce | flops 1 | bytes 8 | tf_op jit(solution)/shard_map/psum | solution.py:19
  316.0 15.2 %all-gather.5.cloned.1.call-done = bf16[8,256,256]{2,1,0:T(8,128)(2,1)} async-done(((bf16[2,256,256]{2,1,0:T(8,128)(2,1)}), bf16[8,256,256]{2,1,0:T(8,128)(2,1)}) %all-gather.5.cloned.1.call-update) | async-done | bytes 1048592 | tf_op jit(solution)/shard_map/all_gather | solution.py:15
  331.3 146.9 %while.29 = (s32[]{:T(128)}, f32[2,256,256]{2,1,0:T(8,128)S(1)}, s32[16]{0:T(128)S(1)}, s32[]{:T(128)}, bf16[16,256,256]{2,1,0:T(8,128)(2,1)}, /*index=5*/s32[16...) while((s32[]{:T(128)}, f32[2,256,256]{2,1,0:T(8,128)S(1)}, ...), condition=%wide.region_14.15_spmd, body=%wide.region_12.14_spmd.sunk | while | flops 235077664 | bytes 1444100 | solution.py:50
  479.7 71.8 %all-reduce.7.cloned.1.call-done = f32[2,256,256]{2,1,0:T(8,128)} async-done(((f32[2,256,256]{2,1,0:T(8,128)}), f32[2,256,256]{2,1,0:T(8,128)}) %all-reduce.7.cloned.1.call-update) | async-done | bytes 524304 | tf_op jit(solution)/shard_map/psum | solution.py:54
  551.5 2.0 fusion.35
  553.5 6.3 %all-reduce = (f32[]{:T(128)}, f32[]{:T(128)}) all-reduce(f32[]{:T(128)} %get-tuple-element.328, f32[]{:T(128)} %get-tuple-element.327), channel_id=1, replica_groups=mesh['sec'=4,'op'=8] {'sec'}, use_global_device_ids=true, to_apply=%region_19.20 | all-reduce | flops 2 | bytes 16 | tf_op jit(solution)/shard_map/psum | solution.py:19
  (187 shorter events, 176.5 us)
Async XLA Ops:
  7.2 23.0 %all-gather.3.cloned.1.call-start = ((), (), s32[]{:S(2)}) async-start(), calls=%async_computation | async-start | bytes 1310720 | tf_op jit(solution)/shard_map/all_gather | solution.py:15
  10.6 275.8 %all-reduce.5.cloned.1.call-start = ((), (), s32[]{:S(2)}) async-start(), calls=%async_computation.1 | async-start | bytes 1048576 | tf_op jit(solution)/shard_map/psum | solution.py:54
  30.2 256.2 %copy-start.2 = (bf16[2,256,256]{2,1,0:T(8,128)(2,1)S(1)}, bf16[2,256,256]{2,1,0:T(8,128)(2,1)}, u32[]{:S(2)}) copy-start(bf16[2,256,256]{2,1,0:T(8,128)(2,1)} %param.18) | copy-start | bytes 786436
  30.2 256.2 %copy-start.4 = (bf16[2,256,256]{2,1,0:T(8,128)(2,1)S(1)}, bf16[2,256,256]{2,1,0:T(8,128)(2,1)}, u32[]{:S(2)}) copy-start(bf16[2,256,256]{2,1,0:T(8,128)(2,1)} %param.19) | copy-start | bytes 786436
  30.2 265.8 %copy-start.6 = (bf16[2,256,256]{2,1,0:T(8,128)(2,1)S(1)}, bf16[2,256,256]{2,1,0:T(8,128)(2,1)}, u32[]{:S(2)}) copy-start(bf16[2,256,256]{2,1,0:T(8,128)(2,1)} %param.20) | copy-start | bytes 786436
  213.0 0.8 copy-start.1
  213.8 117.4 %all-gather.5.cloned.1.call-start = ((), (), s32[]{:S(2)}) async-start(), calls=%async_computation.2 | async-start | bytes 1310720 | tf_op jit(solution)/shard_map/all_gather | solution.py:15
  286.4 20.3 %copy-start.3 = (f32[2,256,256]{2,1,0:T(8,128)S(1)}, f32[2,256,256]{2,1,0:T(8,128)}, u32[]{:S(2)}) copy-start(f32[2,256,256]{2,1,0:T(8,128)} %all-reduce.5.cloned.1.call-done) | copy-start | bytes 1572868
  298.1 33.2 %copy-start.7 = (s32[3]{0:T(128)S(1)}, s32[3]{0:T(128)}, u32[]{:S(2)}) copy-start(s32[3]{0:T(128)} %get-tuple-element.570) | copy-start | bytes 40
  298.1 33.2 %copy-start.8 = (s32[16]{0:T(128)S(1)}, s32[16]{0:T(128)}, u32[]{:S(2)}) copy-start(s32[16]{0:T(128)} %get-tuple-element.571) | copy-start | bytes 196
  298.1 33.2 %copy-start.9 = (s32[16]{0:T(128)S(1)}, s32[16]{0:T(128)}, u32[]{:S(2)}) copy-start(s32[16]{0:T(128)} %get-tuple-element.572) | copy-start | bytes 196
  315.9 235.6 %all-reduce.7.cloned.1.call-start = ((), (), s32[]{:S(2)}) async-start(), calls=%async_computation.3 | async-start | bytes 1048576 | tf_op jit(solution)/shard_map/psum | solution.py:54
  331.3 220.3 %copy-start.5 = (bf16[2,256,256]{2,1,0:T(8,128)(2,1)S(1)}, bf16[2,256,256]{2,1,0:T(8,128)(2,1)}, u32[]{:S(2)}) copy-start(bf16[2,256,256]{2,1,0:T(8,128)(2,1)} %multiply_convert_fusion) | copy-start | bytes 786436
  478.2 0.8 copy-start
Sparse Core Ops, SparseCore 0:
  10.7 19.4 all-gather.2
  214.0 72.3 all-reduce.4
  316.1 15.1 all-gather.4
  479.1 72.3 all-reduce.6
where the time goes:
time: 573 us; the launch traced here: 569 us
  waiting for transfers between devices  179 us (31%)
  loops' own time  142 us (25%)
  matrix products  95.3 us (17%)
  local copies, waits for them, and re-layouts  62.9 us (11%)
  other arithmetic  44.3 us (8%)
  blocking collectives  26.3 us (5%)
  between operations  19.2 us (3%)
    psum x2, waiting for transfers between devices, sum_pairs(): return lax.psum(partial_value, 'op')  144 us
    another operation x2, loops' own time, pair_partial(): return lax.fori_loop(0, left_operator_blocks.shape[0], add_pair, zero_sum)  142 us
    dot_general x32, matrix products, add_pair(): jnp.dot(middle, right_operator_blocks[slot_index].astype(jnp.float32), pr...  58.4 us
    dot_general x32, matrix products, add_pair(): jnp.dot(left_operator_blocks[slot_index], source_block, preferred_element...  36.9 us
    all_gather x2, waiting for transfers between devices, gather_sources(): return lax.all_gather(own_vector, 'sec', axis=0, tiled=True)  34.8 us
    another operation x32, other arithmetic  33.8 us
    dynamic_slice x32, local copies, waits for them, and re-layouts, add_pair(): return partial_value.at[slot_target_sector[slot_index]].add(contribution)  29.7 us
    dynamic_slice x32, local copies, waits for them, and re-layouts, add_pair(): slot_source_sector[slot_index]  29.3 us
  transfers between devices with their start and end apart: 4, of which 4 were waited for; matrix products, arithmetic and copies ran while one was open for 0% of the time, Pallas kernels for 0%

commit v1 on v0

v1 whole, which is shorter than its diff:
```python
import functools

import jax
import jax.numpy as jnp
from jax import lax
from jax.experimental import pallas as pl
from jax.experimental.pallas import tpu as pltpu
from jax.sharding import PartitionSpec as P

MESH = pl.DeviceIdType.MESH
F32 = jnp.float32
BF16 = jnp.bfloat16


def fold_rows(values):
    sums = jnp.sum(values, axis=0, keepdims=True)
    total = sums[:, :128]
    for start in range(128, values.shape[1], 128):
        total = total + sums[:, start : start + 128]
    return total


def make_message(rows):
    blank = jnp.zeros((8 - len(rows), 128), F32)
    return jnp.concatenate(list(rows) + [blank], axis=0)


def davidson_kernel(
    n_sec, n_op, wave, diag, prec, left, right, source, target, count, left_dims, right_dims,
    corr_out, prod_out, proj_out,
    left_v, right_v, all_v, all_c, vec32, diag32, corr32, partial, wire, rs_first, rs_second,
    op_box, sec_box, load_sem, out_sem,
    v_send, v_recv, v_fsend, v_frecv, r1_send, r1_recv, r2_send, r2_recv,
    c_send, c_recv, cy_send, cy_recv, cf_send, cf_recv, op_send, op_recv, sec_send, sec_recv,
):
    sec, op = lax.axis_index("sec"), lax.axis_index("op")
    count_s, block, width = wave.shape
    slots = left.shape[0]
    n_chip = n_sec // 2
    chip, core = sec // 2, lax.rem(sec, 2)
    sibling = sec + 1 - 2 * core
    flat = count_s * block // n_op
    share = block // n_op
    entries = float(n_sec * count_s * block * width)
    first = sec * count_s

    def rotate(index, step, size):
        return lax.rem(index + step + size, size)

    def remote(src, dst, send, recv, device):
        return pltpu.make_async_remote_copy(
            src_ref=src, dst_ref=dst, send_sem=send, recv_sem=recv,
            device_id=device, device_id_type=MESH,
        )

    loads = [
        pltpu.make_async_copy(left, left_v, load_sem.at[0]),
        pltpu.make_async_copy(right, right_v, load_sem.at[1]),
    ]
    for copy in loads:
        copy.start()

    barrier = pltpu.get_barrier_semaphore()
    for step in range(1, n_op):
        pl.semaphore_signal(
            barrier, inc=1, device_id=(sec, rotate(op, step, n_op)), device_id_type=MESH
        )
    for step in range(1, n_sec):
        pl.semaphore_signal(
            barrier, inc=1, device_id=(rotate(sec, step, n_sec), op), device_id_type=MESH
        )

    def used_mask(sector, row_start, rows):
        row = lax.broadcasted_iota(jnp.int32, (rows, width), 0) + row_start
        col = lax.broadcasted_iota(jnp.int32, (rows, width), 1)
        return (row < left_dims[first + sector]) & (col < right_dims[first + sector])

    for t in range(count_s):
        masked = jnp.where(used_mask(t, 0, block), wave[t].astype(F32), 0.0)
        vec32[t] = masked
        all_v[first + t] = masked.astype(BF16)

    pl.semaphore_wait(barrier, n_op - 1 + n_sec - 1)

    sends = []
    for t in range(count_s):
        for step in range(1, n_chip):
            other = rotate(chip, step, n_chip) * 2 + core
            spot = all_v.at[first + t]
            copy = remote(spot, spot, v_send.at[step, t], v_recv.at[step, t], (other, op))
            copy.start()
            sends.append(copy)
    for t in range(count_s):
        spot = all_v.at[first + t]
        copy = remote(spot, spot, v_fsend.at[0, t], v_frecv.at[0, t], (sibling, op))
        copy.start()
        sends.append(copy)
    for t in range(count_s):
        diag32[t] = diag[t].astype(F32)
    for copy in loads:
        copy.wait()
    for t in range(count_s):
        for step in range(1, n_chip):
            origin = rotate(chip, -step, n_chip) * 2 + core
            spot = all_v.at[origin * count_s + t]
            remote(spot, spot, v_send.at[step, t], v_recv.at[step, t], (origin, op)).wait_recv()
            copy = remote(spot, spot, v_fsend.at[step, t], v_frecv.at[step, t], (sibling, op))
            copy.start()
            sends.append(copy)
    for t in range(count_s):
        for step in range(n_chip):
            origin = rotate(chip, -step, n_chip) * 2 + 1 - core
            spot = all_v.at[origin * count_s + t]
            remote(
                spot, spot, v_fsend.at[step, t], v_frecv.at[step, t], (sibling, op)
            ).wait_recv()

    half = block // 2
    group = 4 if slots % 4 == 0 else 1

    def apply_rows(field, row_start):
        for t in range(count_s):
            partial[t, row_start : row_start + half] = jnp.zeros((half, width), F32)

        def some_slots(index, carry):
            sums = [None] * count_s
            for u in range(group):
                k = index * group + u
                live = k < count[0]
                middle = jnp.dot(
                    left_v[k, row_start : row_start + half], field[source[k]],
                    preferred_element_type=F32,
                )
                high = middle.astype(BF16)
                low = (middle - high.astype(F32)).astype(BF16)
                both = jnp.dot(
                    jnp.concatenate([high, low], axis=0), right_v[k],
                    preferred_element_type=F32,
                )
                product = both[:half] + both[half:]
                for t in range(count_s):
                    weight = jnp.where(live & (target[k] == t), 1.0, 0.0).astype(F32)
                    term = product * weight
                    sums[t] = term if sums[t] is None else sums[t] + term
            for t in range(count_s):
                partial[t, row_start : row_start + half] += sums[t]
            return carry

        lax.fori_loop(0, slots // group, some_slots, 0)

    def exchange(turn, rows):
        message = make_message(rows)
        copies = []
        mine = op_box.at[turn, op]
        op_box[turn, op] = message
        for step in range(1, n_op):
            copy = remote(
                mine, mine, op_send.at[turn, step], op_recv.at[turn, step],
                (sec, rotate(op, step, n_op)),
            )
            copy.start()
            copies.append(copy)
        for step in range(1, n_op):
            origin = rotate(op, -step, n_op)
            spot = op_box.at[turn, origin]
            remote(
                spot, spot, op_send.at[turn, step], op_recv.at[turn, step], (sec, origin)
            ).wait_recv()
        total = op_box[turn, 0]
        for index in range(1, n_op):
            total = total + op_box[turn, index]
        mine = sec_box.at[turn, sec]
        sec_box[turn, sec] = total
        for step in range(1, n_sec):
            copy = remote(
                mine, mine, sec_send.at[turn, step], sec_recv.at[turn, step],
                (rotate(sec, step, n_sec), op),
            )
            copy.start()
            copies.append(copy)
        for step in range(1, n_sec):
            origin = rotate(sec, -step, n_sec)
            spot = sec_box.at[turn, origin]
            remote(
                spot, spot, sec_send.at[turn, step], sec_recv.at[turn, step], (origin, op)
            ).wait_recv()
        total = sec_box[turn, 0]
        for index in range(1, n_sec):
            total = total + sec_box[turn, index]
        for copy in copies:
            copy.wait_send()
        return jnp.sum(total, axis=1, keepdims=True)

    def first_copy(dest):
        spot = partial.at[dest * flat // block, pl.ds(dest * flat % block, flat)]
        return remote(spot, rs_first.at[op], r1_send.at[dest], r1_recv.at[op], (sec, dest))

    for part in range(2):
        apply_rows(all_v, part * half)
        for dest in range(n_op):
            if dest * flat % block // half == part:

                @pl.when(dest != op)
                def _():
                    first_copy(dest).start()

    own_sector = op * flat // block
    own_row = pl.multiple_of(lax.rem(op * flat, block), flat)
    own_rows = pl.ds(own_row, flat)
    pairs = partial[own_sector, own_rows]
    for step in range(1, n_op):
        origin = rotate(op, -step, n_op)
        spot = rs_first.at[origin]
        remote(spot, spot, r1_send.at[origin], r1_recv.at[origin], (sec, origin)).wait_recv()
        pairs = pairs + rs_first[origin]

    vector = vec32[own_sector, own_rows]
    scale = prec[own_sector, own_rows].astype(F32)
    sigma = diag32[own_sector, own_rows] * vector + pairs
    sigma = jnp.where(used_mask(own_sector, own_row, flat), sigma, 0.0)
    scaled_vector = scale * vector
    sums = exchange(
        0,
        [
            fold_rows(vector * vector),
            fold_rows(vector * sigma),
            fold_rows(scaled_vector * sigma),
            fold_rows(scaled_vector * vector),
        ],
    )
    norm_vector = sums[0:1]
    rayleigh = sums[1:2] / norm_vector
    along_vector = sums[2:3] - rayleigh * sums[3:4]
    orthogonal = scale * (sigma - rayleigh * vector) - along_vector / norm_vector * vector
    square_norm = exchange(1, [fold_rows(orthogonal * orthogonal)])[0:1]
    correction = orthogonal * lax.rsqrt(square_norm / entries + 1e-06)
    all_c[first + own_sector, own_rows] = correction.astype(BF16)

    def share_of(owner_sec, owner_op):
        row = pl.multiple_of(lax.rem(owner_op * flat, block), flat)
        return all_c.at[owner_sec * count_s + owner_op * flat // block, pl.ds(row, flat)]

    mine = share_of(sec, op)
    for step in range(1, n_op):
        copy = remote(
            mine, mine, c_send.at[step], c_recv.at[step], (sec, rotate(op, step, n_op))
        )
        copy.start()
        sends.append(copy)
    for step in range(n_op):
        origin = rotate(op, -step, n_op)
        spot = share_of(sec, origin)
        if step:
            remote(spot, spot, c_send.at[step], c_recv.at[step], (sec, origin)).wait_recv()
        for jump in range(1, n_chip):
            other = rotate(chip, jump, n_chip) * 2 + core
            copy = remote(
                spot, spot, cy_send.at[jump, step], cy_recv.at[jump, step], (other, op)
            )
            copy.start()
            sends.append(copy)

    def whole_of(owner_sec):
        return all_c.at[pl.ds(owner_sec * count_s, count_s)]

    spot = whole_of(sec)
    copy = remote(spot, spot, cf_send.at[0], cf_recv.at[0], (sibling, op))
    copy.start()
    sends.append(copy)
    out_copy = pltpu.make_async_copy(spot, corr_out, out_sem)
    out_copy.start()
    for t in range(count_s):
        corr32[t] = all_c[first + t].astype(F32)
    for dest in range(n_op):

        @pl.when(dest != op)
        def _():
            first_copy(dest).wait_send()

    for jump in range(1, n_chip):
        owner = rotate(chip, -jump, n_chip) * 2 + core
        for step in range(n_op):
            origin = rotate(op, -step, n_op)
            spot = share_of(owner, origin)
            remote(
                spot, spot, cy_send.at[jump, step], cy_recv.at[jump, step], (owner, op)
            ).wait_recv()
        spot = whole_of(owner)
        copy = remote(spot, spot, cf_send.at[jump], cf_recv.at[jump], (sibling, op))
        copy.start()
        sends.append(copy)
    for jump in range(n_chip):
        owner = rotate(chip, -jump, n_chip) * 2 + 1 - core
        spot = whole_of(owner)
        remote(spot, spot, cf_send.at[jump], cf_recv.at[jump], (sibling, op)).wait_recv()

    narrow = wire is not None
    outgoing = wire if narrow else partial

    def second_copy(dest):
        spot = outgoing.at[:, pl.ds(dest * share, share)]
        return remote(spot, rs_second.at[op], r2_send.at[dest], r2_recv.at[op], (sec, dest))

    for part in range(2):
        apply_rows(all_c, part * half)
        if narrow:
            for t in range(count_s):
                wire[t, part * half : part * half + half] = partial[
                    t, part * half : part * half + half
                ].astype(BF16)
        for dest in range(n_op):
            if dest * share // half == part:

                @pl.when(dest != op)
                def _():
                    second_copy(dest).start()

    share_row = pl.multiple_of(op * share, share)
    share_rows = pl.ds(share_row, share)
    pairs = [partial[t, share_rows] for t in range(count_s)]
    for step in range(1, n_op):
        origin = rotate(op, -step, n_op)
        spot = rs_second.at[origin]
        remote(spot, spot, r2_send.at[origin], r2_recv.at[origin], (sec, origin)).wait_recv()
        for t in range(count_s):
            pairs[t] = pairs[t] + rs_second[origin, t].astype(F32)
    cross, self_sum = None, None
    for t in range(count_s):
        field = corr32[t, share_rows]
        product = diag32[t, share_rows] * field + pairs[t]
        product = jnp.where(used_mask(t, share_row, share), product, 0.0)
        prod_out[t] = product
        cross_part = fold_rows(vec32[t, share_rows] * product)
        self_part = fold_rows(field * product)
        cross = cross_part if t == 0 else cross + cross_part
        self_sum = self_part if t == 0 else self_sum + self_part
    sums = exchange(2, [cross, self_sum])
    proj_out[0] = jnp.sum(rayleigh)
    proj_out[1] = jnp.sum(sums[0:1] * lax.rsqrt(norm_vector * entries))
    proj_out[2] = jnp.sum(sums[1:2] / entries)

    for dest in range(n_op):

        @pl.when(dest != op)
        def _():
            second_copy(dest).wait_send()

    for copy in sends:
        copy.wait_send()
    out_copy.wait()


def on_device(n_sec, n_op, wave, diag, prec, left, right, source, target, count, ldims, rdims):
    count_s, block, width = wave.shape
    slots = left.shape[0]
    sectors = n_sec * count_s
    n_chip = n_sec // 2
    flat = count_s * block // n_op
    share = block // n_op
    narrow = share % 16 == 0
    wire_type = BF16 if narrow else F32
    vmem = pl.BlockSpec(memory_space=pltpu.VMEM)
    smem = pl.BlockSpec(memory_space=pltpu.SMEM)
    hbm = pl.BlockSpec(memory_space=pl.ANY)
    dma = pltpu.SemaphoreType.DMA
    scratch = [
        pltpu.VMEM((slots, block, block), BF16),
        pltpu.VMEM((slots, width, width), BF16),
        pltpu.VMEM((sectors, block, width), BF16),
        pltpu.VMEM((sectors, block, width), BF16),
        pltpu.VMEM((count_s, block, width), F32),
        pltpu.VMEM((count_s, block, width), F32),
        pltpu.VMEM((count_s, block, width), F32),
        pltpu.VMEM((count_s, block, width), F32),
    ]
    if narrow:
        scratch.append(pltpu.VMEM((count_s, block, width), BF16))
    scratch += [
        pltpu.VMEM((n_op, flat, width), F32),
        pltpu.VMEM((n_op, count_s, share, width), wire_type),
        pltpu.VMEM((3, n_op, 8, 128), F32),
        pltpu.VMEM((3, n_sec, 8, 128), F32),
        dma((2,)), dma,
        dma((n_chip, count_s)), dma((n_chip, count_s)),
        dma((n_chip, count_s)), dma((n_chip, count_s)),
        dma((n_op,)), dma((n_op,)), dma((n_op,)), dma((n_op,)),
        dma((n_op,)), dma((n_op,)), dma((n_chip, n_op)), dma((n_chip, n_op)),
        dma((n_chip,)), dma((n_chip,)),
        dma((3, n_op)), dma((3, n_op)), dma((3, n_sec)), dma((3, n_sec)),
    ]

    def body(*refs):
        refs = list(refs)
        if not narrow:
            refs.insert(21, None)
        davidson_kernel(n_sec, n_op, *refs)

    return pl.pallas_call(
        body,
        name="davidson_step",
        out_shape=(
            jax.ShapeDtypeStruct((count_s, block, width), BF16),
            jax.ShapeDtypeStruct((count_s, share, width), F32),
            jax.ShapeDtypeStruct((3,), F32),
        ),
        in_specs=[vmem, vmem, vmem, hbm, hbm, smem, smem, smem, smem, smem],
        out_specs=(hbm, vmem, smem),
        scratch_shapes=scratch,
        compiler_params=pltpu.CompilerParams(
            collective_id=0, has_side_effects=True, vmem_limit_bytes=40 * 1024 * 1024
        ),
        cost_estimate=pl.CostEstimate(
            flops=2 * slots * 6 * block * block * width,
            bytes_accessed=4 * slots * block * block,
            transcendentals=0,
        ),
    )(wave, diag, prec, left, right, source, target, count, ldims, rdims)


def solution(mesh):
    split = P(("sec", "op"))
    in_specs = (
        P("sec", None, None),
        P("sec", None, None),
        P("sec", None, None),
        P(("sec", "op"), None, None),
        P(("sec", "op"), None, None),
        split,
        split,
        split,
        P(),
        P(),
    )
    out_specs = (P("sec", None, None), P("sec", "op", None), P())
    return jax.shard_map(
        functools.partial(on_device, mesh.shape["sec"], mesh.shape["op"]),
        mesh=mesh, in_specs=in_specs, out_specs=out_specs, check_vma=False,
    )
```

time: 573 us -> 90.3 us (0.16)
  waiting for transfers between devices: 179 us -> 0 us
  loops' own time: 142 us -> 0 us
  matrix products: 95.3 us -> 0 us
  Pallas kernels: 0 us -> 78.2 us
  local copies, waits for them, and re-layouts: 62.9 us -> 10.5 us
  other arithmetic: 44.3 us -> 0 us
  blocking collectives: 26.3 us -> 0 us
  between operations: 19.2 us -> 1.31 us
    psum x2 -> x0, waiting for transfers between devices: 144 us -> none  [sum_pairs(): return lax.psum(partial_value, 'op')]
    another operation x2 -> x0, loops' own time: 142 us -> none  [pair_partial(): return lax.fori_loop(0, left_operator_blocks.shape[0], add_pair, zero_sum)]
    dot_general x64 -> x0, matrix products: 95.3 us -> none  [the longest x32 58.4 us: add_pair(): jnp.dot(middle, right_operator_blocks[slot_index].astype(jnp.float32), pr...]
    pallas_call x0 -> x1, Pallas kernels: none -> 78.2 us  [on_device(): pl.pallas_call(body, name='davidson_step', out_shape=(jax.ShapeDtypeStruc...]
    dynamic_slice x67 -> x0, local copies, waits for them, and re-layouts: 61.2 us -> none  [the longest x32 29.7 us: add_pair(): return partial_value.at[slot_target_sector[slot_index]].add(contribution)]
    all_gather x2 -> x0, waiting for transfers between devices: 34.8 us -> none  [gather_sources(): return lax.all_gather(own_vector, 'sec', axis=0, tiled=True)]
    another operation x33 -> x0, other arithmetic: 34.3 us -> none
    psum x4 -> x0, blocking collectives: 26.3 us -> none  [reduce_dots(): return lax.psum(values, 'sec')]
  transfers between devices with their start and end apart: 4 -> 0, of which waited for: 4 -> 0; matrix products, arithmetic and copies ran while one was open for 0% -> 0% of each run, Pallas kernels for 0% -> 0%
where the time goes in v1:
time: 90.3 us; the launch traced here: 90 us
  Pallas kernels  78.2 us (87%)
  local copies, waits for them, and re-layouts  10.5 us (12%)
  between operations  1.31 us (1%)
    pallas_call x1, Pallas kernels, on_device(): pl.pallas_call(body, name='davidson_step', out_shape=(jax.ShapeDtypeStruc...  78.2 us
    unnamed x21, local copies, waits for them, and re-layouts  10.5 us

profile of v1, /device:TPU:0, one launch (start us, length us, event | category | flops | bytes accessed | tf_op | source)
XLA Modules:
  0.0 90.0 jit_solution(12893448030422586839)
XLA Ops:
  1.3 0.0 copy-start
  1.3 1.6 %copy-done = bf16[16,256,256]{2,1,0:T(8,128)(2,1)S(1)} copy-done((bf16[16,256,256]{2,1,0:T(8,128)(2,1)S(1)}, bf16[16,256,256]{2,1,0:T(8,128)(2,1)}, u32[]{:S(2)}) %copy-start) | copy-done | bytes 2097176
  2.9 0.0 copy-start.1
  2.9 1.6 %copy-done.1 = bf16[16,256,256]{2,1,0:T(8,128)(2,1)S(1)} copy-done((bf16[16,256,256]{2,1,0:T(8,128)(2,1)S(1)}, bf16[16,256,256]{2,1,0:T(8,128)(2,1)}, u32[]{:S(2)}) %copy-start.1) | copy-done | bytes 2097176
  4.5 0.0 copy-start.2
  4.5 0.9 %copy-done.2 = bf16[2,256,256]{2,1,0:T(8,128)(2,1)S(1)} copy-done((bf16[2,256,256]{2,1,0:T(8,128)(2,1)S(1)}, bf16[2,256,256]{2,1,0:T(8,128)(2,1)}, u32[]{:S(2)}) %copy-start.2) | copy-done | bytes 262168
  5.4 0.0 copy-start.3
  5.4 0.9 %copy-done.3 = bf16[2,256,256]{2,1,0:T(8,128)(2,1)S(1)} copy-done((bf16[2,256,256]{2,1,0:T(8,128)(2,1)S(1)}, bf16[2,256,256]{2,1,0:T(8,128)(2,1)}, u32[]{:S(2)}) %copy-start.3) | copy-done | bytes 262168
  6.4 0.0 copy-start.4
  6.4 0.9 %copy-done.4 = bf16[2,256,256]{2,1,0:T(8,128)(2,1)S(1)} copy-done((bf16[2,256,256]{2,1,0:T(8,128)(2,1)S(1)}, bf16[2,256,256]{2,1,0:T(8,128)(2,1)}, u32[]{:S(2)}) %copy-start.4) | copy-done | bytes 262168
  7.3 0.0 copy-start.5
  7.3 0.7 copy-done.5
  8.0 0.0 copy-start.6
  8.0 0.7 copy-done.6
  8.6 0.0 copy-start.7
  8.6 0.7 copy-done.7
  9.3 0.0 copy-start.8
  9.3 0.7 copy-done.8
  9.9 78.2 %davidson_step.1 = (bf16[2,256,256]{2,1,0:T(8,128)(2,1)S(1)}, f32[2,32,256]{2,1,0:T(8,128)S(1)}, f32[3]{0:T(128)S(1)}) custom-call(bf16[2,256,256]{2,1,0:T(8,128)(2,1)S(1)} %copy-done.2, bf16[2,256,256]{2,1,0:T(8,128)(2,1)S(1)} %copy-done.3, bf16[2,256,256]{2,1,0:T(8,128)(2,1)S(1)} %copy-done.4, bf16[16,256,256]{2,1,0:T(8,128)(2,1)S(1)} %copy-done, ...), custom_call_target="tpu_custom_call" | custom-call | flops 3221225472 | bytes 4194304 | tf_op jit(solution)/shard_map/davidson_step/pallas_call | solution.py:398
  88.2 0.7 copy.17
  88.9 0.6 copy.18
  89.5 0.5 copy.19
Async XLA Ops:
  1.3 1.6 %copy-start = (bf16[16,256,256]{2,1,0:T(8,128)(2,1)S(1)}, bf16[16,256,256]{2,1,0:T(8,128)(2,1)}, u32[]{:S(2)}) copy-start(bf16[16,256,256]{2,1,0:T(8,128)(2,1)} %refs_3_.1) | copy-start | bytes 6291460
  2.9 1.6 %copy-start.1 = (bf16[16,256,256]{2,1,0:T(8,128)(2,1)S(1)}, bf16[16,256,256]{2,1,0:T(8,128)(2,1)}, u32[]{:S(2)}) copy-start(bf16[16,256,256]{2,1,0:T(8,128)(2,1)} %refs_4_.1) | copy-start | bytes 6291460
  4.5 0.9 %copy-start.2 = (bf16[2,256,256]{2,1,0:T(8,128)(2,1)S(1)}, bf16[2,256,256]{2,1,0:T(8,128)(2,1)}, u32[]{:S(2)}) copy-start(bf16[2,256,256]{2,1,0:T(8,128)(2,1)} %refs_0_.1) | copy-start | bytes 786436
  5.4 0.9 %copy-start.3 = (bf16[2,256,256]{2,1,0:T(8,128)(2,1)S(1)}, bf16[2,256,256]{2,1,0:T(8,128)(2,1)}, u32[]{:S(2)}) copy-start(bf16[2,256,256]{2,1,0:T(8,128)(2,1)} %refs_1_.1) | copy-start | bytes 786436
  6.4 0.9 %copy-start.4 = (bf16[2,256,256]{2,1,0:T(8,128)(2,1)S(1)}, bf16[2,256,256]{2,1,0:T(8,128)(2,1)}, u32[]{:S(2)}) copy-start(bf16[2,256,256]{2,1,0:T(8,128)(2,1)} %refs_2_.1) | copy-start | bytes 786436
  7.3 0.7 copy-start.5
  8.0 0.7 copy-start.6
  8.6 0.7 copy-start.7
  9.3 0.7 copy-start.8

commit v2 on v1

--- a/solution.py
+++ b/solution.py
@@ -26,15 +26,16 @@
 
 
 def davidson_kernel(
-    n_sec, n_op, wave, diag, prec, left, right, source, target, count, left_dims, right_dims,
+    n_sec, n_op, wave_h, diag_h, prec_h, left, right, source_h, target_h, count_h, ldims_h, rdims_h,
     corr_out, prod_out, proj_out,
     left_v, right_v, all_v, all_c, vec32, diag32, corr32, partial, wire, rs_first, rs_second,
+    middles, wave, diag, prec, source, target, count, left_dims, right_dims,
     op_box, sec_box, load_sem, out_sem,
     v_send, v_recv, v_fsend, v_frecv, r1_send, r1_recv, r2_send, r2_recv,
     c_send, c_recv, cy_send, cy_recv, cf_send, cf_recv, op_send, op_recv, sec_send, sec_recv,
 ):
     sec, op = lax.axis_index("sec"), lax.axis_index("op")
-    count_s, block, width = wave.shape
+    count_s, block, width = wave_h.shape
     slots = left.shape[0]
     n_chip = n_sec // 2
     chip, core = sec // 2, lax.rem(sec, 2)
@@ -53,9 +54,14 @@
             device_id=device, device_id_type=MESH,
         )
 
+    pairs_in = [
+        (wave_h, wave), (ldims_h, left_dims), (rdims_h, right_dims), (source_h, source),
+        (target_h, target), (count_h, count), (diag_h, diag), (prec_h, prec),
+        (left, left_v), (right, right_v),
+    ]
     loads = [
-        pltpu.make_async_copy(left, left_v, load_sem.at[0]),
-        pltpu.make_async_copy(right, right_v, load_sem.at[1]),
+        pltpu.make_async_copy(src, dst, load_sem.at[index])
+        for index, (src, dst) in enumerate(pairs_in)
     ]
     for copy in loads:
         copy.start()
@@ -70,6 +76,9 @@
             barrier, inc=1, device_id=(rotate(sec, step, n_sec), op), device_id_type=MESH
         )
 
+    for copy in loads[:3]:
+        copy.wait()
+
     def used_mask(sector, row_start, rows):
         row = lax.broadcasted_iota(jnp.int32, (rows, width), 0) + row_start
         col = lax.broadcasted_iota(jnp.int32, (rows, width), 1)
@@ -95,10 +104,10 @@
         copy = remote(spot, spot, v_fsend.at[0, t], v_frecv.at[0, t], (sibling, op))
         copy.start()
         sends.append(copy)
+    for copy in loads[3:]:
+        copy.wait()
     for t in range(count_s):
         diag32[t] = diag[t].astype(F32)
-    for copy in loads:
-        copy.wait()
     for t in range(count_s):
         for step in range(1, n_chip):
             origin = rotate(chip, -step, n_chip) * 2 + core
@@ -118,7 +127,23 @@
     half = block // 2
     group = 4 if slots % 4 == 0 else 1
 
-    def apply_rows(field, row_start):
+    def fill_middles(field):
+        def some_slots(index, carry):
+            for u in range(group):
+                k = index * group + u
+                middle = jnp.dot(left_v[k], field[source[k]], preferred_element_type=F32)
+                high = middle.astype(BF16)
+                low = (middle - high.astype(F32)).astype(BF16)
+                for part in range(2):
+                    rows = slice(part * half, part * half + half)
+                    middles[k, part, :half] = high[rows]
+                    middles[k, part, half:] = low[rows]
+            return carry
+
+        lax.fori_loop(0, slots // group, some_slots, 0)
+
+    def apply_rows(part):
+        row_start = part * half
         for t in range(count_s):
             partial[t, row_start : row_start + half] = jnp.zeros((half, width), F32)
 
@@ -127,16 +152,7 @@
             for u in range(group):
                 k = index * group + u
                 live = k < count[0]
-                middle = jnp.dot(
-                    left_v[k, row_start : row_start + half], field[source[k]],
-                    preferred_element_type=F32,
-                )
-                high = middle.astype(BF16)
-                low = (middle - high.astype(F32)).astype(BF16)
-                both = jnp.dot(
-                    jnp.concatenate([high, low], axis=0), right_v[k],
-                    preferred_element_type=F32,
-                )
+                both = jnp.dot(middles[k, part], right_v[k], preferred_element_type=F32)
                 product = both[:half] + both[half:]
                 for t in range(count_s):
                     weight = jnp.where(live & (target[k] == t), 1.0, 0.0).astype(F32)
@@ -195,8 +211,9 @@
         spot = partial.at[dest * flat // block, pl.ds(dest * flat % block, flat)]
         return remote(spot, rs_first.at[op], r1_send.at[dest], r1_recv.at[op], (sec, dest))
 
+    fill_middles(all_v)
     for part in range(2):
-        apply_rows(all_v, part * half)
+        apply_rows(part)
         for dest in range(n_op):
             if dest * flat % block // half == part:
 
@@ -207,30 +224,37 @@
     own_sector = op * flat // block
     own_row = pl.multiple_of(lax.rem(op * flat, block), flat)
     own_rows = pl.ds(own_row, flat)
+    vector = vec32[own_sector, own_rows]
+    scale = prec[own_sector, own_rows].astype(F32)
+    scaled_vector = scale * vector
+    local = diag32[own_sector, own_rows] * vector
+
+    with_vector = fold_rows(vector * local)
+    with_scaled = fold_rows(scaled_vector * local)
+    for t in range(count_s):
+        weighted = vec32[t] * partial[t]
+        with_vector = with_vector + fold_rows(weighted)
+        with_scaled = with_scaled + fold_rows(weighted * prec[t].astype(F32))
+    sums = exchange(
+        0,
+        [
+            fold_rows(vector * vector),
+            with_vector,
+            with_scaled,
+            fold_rows(scaled_vector * vector),
+        ],
+    )
+    norm_vector = sums[0:1]
+    rayleigh = sums[1:2] / norm_vector
+    along_vector = sums[2:3] - rayleigh * sums[3:4]
+
     pairs = partial[own_sector, own_rows]
     for step in range(1, n_op):
         origin = rotate(op, -step, n_op)
         spot = rs_first.at[origin]
         remote(spot, spot, r1_send.at[origin], r1_recv.at[origin], (sec, origin)).wait_recv()
         pairs = pairs + rs_first[origin]
-
-    vector = vec32[own_sector, own_rows]
-    scale = prec[own_sector, own_rows].astype(F32)
-    sigma = diag32[own_sector, own_rows] * vector + pairs
-    sigma = jnp.where(used_mask(own_sector, own_row, flat), sigma, 0.0)
-    scaled_vector = scale * vector
-    sums = exchange(
-        0,
-        [
-            fold_rows(vector * vector),
-            fold_rows(vector * sigma),
-            fold_rows(scaled_vector * sigma),
-            fold_rows(scaled_vector * vector),
-        ],
-    )
-    norm_vector = sums[0:1]
-    rayleigh = sums[1:2] / norm_vector
-    along_vector = sums[2:3] - rayleigh * sums[3:4]
+    sigma = jnp.where(used_mask(own_sector, own_row, flat), local + pairs, 0.0)
     orthogonal = scale * (sigma - rayleigh * vector) - along_vector / norm_vector * vector
     square_norm = exchange(1, [fold_rows(orthogonal * orthogonal)])[0:1]
     correction = orthogonal * lax.rsqrt(square_norm / entries + 1e-06)
@@ -301,8 +325,9 @@
         spot = outgoing.at[:, pl.ds(dest * share, share)]
         return remote(spot, rs_second.at[op], r2_send.at[dest], r2_recv.at[op], (sec, dest))
 
+    fill_middles(all_c)
     for part in range(2):
-        apply_rows(all_c, part * half)
+        apply_rows(part)
         if narrow:
             for t in range(count_s):
                 wire[t, part * half : part * half + half] = partial[
@@ -317,6 +342,16 @@
 
     share_row = pl.multiple_of(op * share, share)
     share_rows = pl.ds(share_row, share)
+    cross = jnp.zeros((1, 128), F32)
+    self_sum = jnp.zeros((1, 128), F32)
+    local = []
+    for t in range(count_s):
+        field = corr32[t, share_rows]
+        own = diag32[t, share_rows] * field
+        local.append(own)
+        cross = cross + fold_rows(vec32[t] * partial[t]) + fold_rows(vec32[t, share_rows] * own)
+        self_sum = self_sum + fold_rows(corr32[t] * partial[t]) + fold_rows(field * own)
+    sums = exchange(2, [cross, self_sum])
     pairs = [partial[t, share_rows] for t in range(count_s)]
     for step in range(1, n_op):
         origin = rotate(op, -step, n_op)
@@ -324,17 +359,9 @@
         remote(spot, spot, r2_send.at[origin], r2_recv.at[origin], (sec, origin)).wait_recv()
         for t in range(count_s):
             pairs[t] = pairs[t] + rs_second[origin, t].astype(F32)
-    cross, self_sum = None, None
-    for t in range(count_s):
-        field = corr32[t, share_rows]
-        product = diag32[t, share_rows] * field + pairs[t]
-        product = jnp.where(used_mask(t, share_row, share), product, 0.0)
-        prod_out[t] = product
-        cross_part = fold_rows(vec32[t, share_rows] * product)
-        self_part = fold_rows(field * product)
-        cross = cross_part if t == 0 else cross + cross_part
-        self_sum = self_part if t == 0 else self_sum + self_part
-    sums = exchange(2, [cross, self_sum])
+    for t in range(count_s):
+        mask = used_mask(t, share_row, share)
+        prod_out[t] = jnp.where(mask, local[t] + pairs[t], 0.0)
     proj_out[0] = jnp.sum(rayleigh)
     proj_out[1] = jnp.sum(sums[0:1] * lax.rsqrt(norm_vector * entries))
     proj_out[2] = jnp.sum(sums[1:2] / entries)
@@ -361,7 +388,7 @@
     wire_type = BF16 if narrow else F32
     vmem = pl.BlockSpec(memory_space=pltpu.VMEM)
     smem = pl.BlockSpec(memory_space=pltpu.SMEM)
-    hbm = pl.BlockSpec(memory_space=pl.ANY)
+    hbm = pl.BlockSpec(memory_space=pltpu.HBM)
     dma = pltpu.SemaphoreType.DMA
     scratch = [
         pltpu.VMEM((slots, block, block), BF16),
@@ -378,9 +405,18 @@
     scratch += [
         pltpu.VMEM((n_op, flat, width), F32),
         pltpu.VMEM((n_op, count_s, share, width), wire_type),
+        pltpu.VMEM((slots, 2, block, width), BF16),
+        pltpu.VMEM((count_s, block, width), BF16),
+        pltpu.VMEM((count_s, block, width), BF16),
+        pltpu.VMEM((count_s, block, width), BF16),
+        pltpu.SMEM(source.shape, jnp.int32),
+        pltpu.SMEM(target.shape, jnp.int32),
+        pltpu.SMEM(count.shape, jnp.int32),
+        pltpu.SMEM(ldims.shape, jnp.int32),
+        pltpu.SMEM(rdims.shape, jnp.int32),
         pltpu.VMEM((3, n_op, 8, 128), F32),
         pltpu.VMEM((3, n_sec, 8, 128), F32),
-        dma((2,)), dma,
+        dma((10,)), dma,
         dma((n_chip, count_s)), dma((n_chip, count_s)),
         dma((n_chip, count_s)), dma((n_chip, count_s)),
         dma((n_op,)), dma((n_op,)), dma((n_op,)), dma((n_op,)),
@@ -403,7 +439,7 @@
             jax.ShapeDtypeStruct((count_s, share, width), F32),
             jax.ShapeDtypeStruct((3,), F32),
         ),
-        in_specs=[vmem, vmem, vmem, hbm, hbm, smem, smem, smem, smem, smem],
+        in_specs=[hbm] * 10,
         out_specs=(hbm, vmem, smem),
         scratch_shapes=scratch,
         compiler_params=pltpu.CompilerParams(

time: 90.3 us -> 79.3 us (0.88)
  Pallas kernels: 78.2 us -> 67.2 us
    pallas_call x1, Pallas kernels: 78.2 us -> 67.2 us  [on_device(): pl.pallas_call(body, name='davidson_step', out_shape=(jax.ShapeDtypeStruc...]
where the time goes in v2:
time: 79.3 us; the launch traced here: 79 us
  Pallas kernels  67.2 us (85%)
  local copies, waits for them, and re-layouts  10.5 us (13%)
  between operations  1.31 us (2%)
    pallas_call x1, Pallas kernels, on_device(): pl.pallas_call(body, name='davidson_step', out_shape=(jax.ShapeDtypeStruc...  67.2 us
    unnamed x21, local copies, waits for them, and re-layouts  10.5 us

profile of v2, /device:TPU:0, one launch (start us, length us, event | category | flops | bytes accessed | tf_op | source)
XLA Modules:
  0.0 79.0 jit_solution(15915162420585578001)
XLA Ops:
  1.3 0.0 copy-start
  1.3 1.6 %copy-done = bf16[16,256,256]{2,1,0:T(8,128)(2,1)S(1)} copy-done((bf16[16,256,256]{2,1,0:T(8,128)(2,1)S(1)}, bf16[16,256,256]{2,1,0:T(8,128)(2,1)}, u32[]{:S(2)}) %copy-start) | copy-done | bytes 2097176
  2.9 0.0 copy-start.1
  2.9 1.6 %copy-done.1 = bf16[16,256,256]{2,1,0:T(8,128)(2,1)S(1)} copy-done((bf16[16,256,256]{2,1,0:T(8,128)(2,1)S(1)}, bf16[16,256,256]{2,1,0:T(8,128)(2,1)}, u32[]{:S(2)}) %copy-start.1) | copy-done | bytes 2097176
  4.5 0.0 copy-start.2
  4.5 0.9 %copy-done.2 = bf16[2,256,256]{2,1,0:T(8,128)(2,1)S(1)} copy-done((bf16[2,256,256]{2,1,0:T(8,128)(2,1)S(1)}, bf16[2,256,256]{2,1,0:T(8,128)(2,1)}, u32[]{:S(2)}) %copy-start.2) | copy-done | bytes 262168
  5.4 0.0 copy-start.3
  5.4 0.9 %copy-done.3 = bf16[2,256,256]{2,1,0:T(8,128)(2,1)S(1)} copy-done((bf16[2,256,256]{2,1,0:T(8,128)(2,1)S(1)}, bf16[2,256,256]{2,1,0:T(8,128)(2,1)}, u32[]{:S(2)}) %copy-start.3) | copy-done | bytes 262168
  6.4 0.0 copy-start.4
  6.4 0.9 %copy-done.4 = bf16[2,256,256]{2,1,0:T(8,128)(2,1)S(1)} copy-done((bf16[2,256,256]{2,1,0:T(8,128)(2,1)S(1)}, bf16[2,256,256]{2,1,0:T(8,128)(2,1)}, u32[]{:S(2)}) %copy-start.4) | copy-done | bytes 262168
  7.3 0.0 copy-start.5
  7.3 0.7 copy-done.5
  8.0 0.0 copy-start.6
  8.0 0.7 copy-done.6
  8.6 0.0 copy-start.7
  8.6 0.7 copy-done.7
  9.3 0.0 copy-start.8
  9.3 0.7 copy-done.8
  9.9 67.2 %davidson_step.1 = (bf16[2,256,256]{2,1,0:T(8,128)(2,1)S(1)}, f32[2,32,256]{2,1,0:T(8,128)S(1)}, f32[3]{0:T(128)S(1)}) custom-call(bf16[2,256,256]{2,1,0:T(8,128)(2,1)S(1)} %copy-done.2, bf16[2,256,256]{2,1,0:T(8,128)(2,1)S(1)} %copy-done.3, bf16[2,256,256]{2,1,0:T(8,128)(2,1)S(1)} %copy-done.4, bf16[16,256,256]{2,1,0:T(8,128)(2,1)S(1)} %copy-done, ...), custom_call_target="tpu_custom_call" | custom-call | flops 3221225472 | bytes 4194304 | tf_op jit(solution)/shard_map/davidson_step/pallas_call | solution.py:434
  77.1 0.7 copy.17
  77.8 0.6 copy.18
  78.5 0.5 copy.19
Async XLA Ops:
  1.3 1.6 %copy-start = (bf16[16,256,256]{2,1,0:T(8,128)(2,1)S(1)}, bf16[16,256,256]{2,1,0:T(8,128)(2,1)}, u32[]{:S(2)}) copy-start(bf16[16,256,256]{2,1,0:T(8,128)(2,1)} %refs_3_.1) | copy-start | bytes 6291460
  2.9 1.6 %copy-start.1 = (bf16[16,256,256]{2,1,0:T(8,128)(2,1)S(1)}, bf16[16,256,256]{2,1,0:T(8,128)(2,1)}, u32[]{:S(2)}) copy-start(bf16[16,256,256]{2,1,0:T(8,128)(2,1)} %refs_4_.1) | copy-start | bytes 6291460
  4.5 0.9 %copy-start.2 = (bf16[2,256,256]{2,1,0:T(8,128)(2,1)S(1)}, bf16[2,256,256]{2,1,0:T(8,128)(2,1)}, u32[]{:S(2)}) copy-start(bf16[2,256,256]{2,1,0:T(8,128)(2,1)} %refs_0_.1) | copy-start | bytes 786436
  5.4 0.9 %copy-start.3 = (bf16[2,256,256]{2,1,0:T(8,128)(2,1)S(1)}, bf16[2,256,256]{2,1,0:T(8,128)(2,1)}, u32[]{:S(2)}) copy-start(bf16[2,256,256]{2,1,0:T(8,128)(2,1)} %refs_1_.1) | copy-start | bytes 786436
  6.4 0.9 %copy-start.4 = (bf16[2,256,256]{2,1,0:T(8,128)(2,1)S(1)}, bf16[2,256,256]{2,1,0:T(8,128)(2,1)}, u32[]{:S(2)}) copy-start(bf16[2,256,256]{2,1,0:T(8,128)(2,1)} %refs_2_.1) | copy-start | bytes 786436
  7.3 0.7 copy-start.5
  8.0 0.7 copy-start.6
  8.6 0.7 copy-start.7
  9.3 0.7 copy-start.8

commit v3 on v2

--- a/solution.py
+++ b/solution.py
@@ -10,6 +10,8 @@
 MESH = pl.DeviceIdType.MESH
 F32 = jnp.float32
 BF16 = jnp.bfloat16
+VMEM_BYTES = 64 * 1024 * 1024
+DIRECT_DEVICES = 32
 
 
 def fold_rows(values):
@@ -30,7 +32,7 @@
     corr_out, prod_out, proj_out,
     left_v, right_v, all_v, all_c, vec32, diag32, corr32, partial, wire, rs_first, rs_second,
     middles, wave, diag, prec, source, target, count, left_dims, right_dims,
-    op_box, sec_box, load_sem, out_sem,
+    op_box, sec_box, all_box, all_send, all_recv, load_sem, out_sem,
     v_send, v_recv, v_fsend, v_frecv, r1_send, r1_recv, r2_send, r2_recv,
     c_send, c_recv, cy_send, cy_recv, cf_send, cf_recv, op_send, op_recv, sec_send, sec_recv,
 ):
@@ -67,14 +69,19 @@
         copy.start()
 
     barrier = pltpu.get_barrier_semaphore()
-    for step in range(1, n_op):
-        pl.semaphore_signal(
-            barrier, inc=1, device_id=(sec, rotate(op, step, n_op)), device_id_type=MESH
-        )
-    for step in range(1, n_sec):
-        pl.semaphore_signal(
-            barrier, inc=1, device_id=(rotate(sec, step, n_sec), op), device_id_type=MESH
-        )
+    direct = n_sec * n_op <= DIRECT_DEVICES
+    others = [
+        (jump, step)
+        for jump in range(n_sec)
+        for step in range(n_op)
+        if jump + step and (direct or jump * step == 0)
+    ]
+
+    def other(jump, step):
+        return rotate(sec, jump, n_sec), rotate(op, step, n_op)
+
+    for jump, step in others:
+        pl.semaphore_signal(barrier, inc=1, device_id=other(jump, step), device_id_type=MESH)
 
     for copy in loads[:3]:
         copy.wait()
@@ -89,14 +96,14 @@
         vec32[t] = masked
         all_v[first + t] = masked.astype(BF16)
 
-    pl.semaphore_wait(barrier, n_op - 1 + n_sec - 1)
+    pl.semaphore_wait(barrier, len(others))
 
     sends = []
     for t in range(count_s):
         for step in range(1, n_chip):
-            other = rotate(chip, step, n_chip) * 2 + core
+            target_sec = rotate(chip, step, n_chip) * 2 + core
             spot = all_v.at[first + t]
-            copy = remote(spot, spot, v_send.at[step, t], v_recv.at[step, t], (other, op))
+            copy = remote(spot, spot, v_send.at[step, t], v_recv.at[step, t], (target_sec, op))
             copy.start()
             sends.append(copy)
     for t in range(count_s):
@@ -207,6 +214,26 @@
             copy.wait_send()
         return jnp.sum(total, axis=1, keepdims=True)
 
+    def exchange_direct(rows):
+        mine = all_box.at[sec, op]
+        all_box[sec, op] = make_message(rows)
+        for jump, step in others:
+            copy = remote(
+                mine, mine, all_send.at[jump, step], all_recv.at[jump, step], other(jump, step)
+            )
+            copy.start()
+            sends.append(copy)
+        for jump, step in others:
+            origin = other(-jump, -step)
+            spot = all_box.at[origin[0], origin[1]]
+            remote(
+                spot, spot, all_send.at[jump, step], all_recv.at[jump, step], origin
+            ).wait_recv()
+        parts = [all_box[a, b] for a in range(n_sec) for b in range(n_op)]
+        while len(parts) > 1:
+            parts = [parts[i] + parts[i + 1] for i in range(0, len(parts), 2)]
+        return jnp.sum(parts[0], axis=1, keepdims=True)
+
     def first_copy(dest):
         spot = partial.at[dest * flat // block, pl.ds(dest * flat % block, flat)]
         return remote(spot, rs_first.at[op], r1_send.at[dest], r1_recv.at[op], (sec, dest))
@@ -256,7 +283,8 @@
         pairs = pairs + rs_first[origin]
     sigma = jnp.where(used_mask(own_sector, own_row, flat), local + pairs, 0.0)
     orthogonal = scale * (sigma - rayleigh * vector) - along_vector / norm_vector * vector
-    square_norm = exchange(1, [fold_rows(orthogonal * orthogonal)])[0:1]
+    squares = [fold_rows(orthogonal * orthogonal)]
+    square_norm = (exchange_direct(squares) if direct else exchange(1, squares))[0:1]
     correction = orthogonal * lax.rsqrt(square_norm / entries + 1e-06)
     all_c[first + own_sector, own_rows] = correction.astype(BF16)
 
@@ -277,9 +305,9 @@
         if step:
             remote(spot, spot, c_send.at[step], c_recv.at[step], (sec, origin)).wait_recv()
         for jump in range(1, n_chip):
-            other = rotate(chip, jump, n_chip) * 2 + core
+            target_sec = rotate(chip, jump, n_chip) * 2 + core
             copy = remote(
-                spot, spot, cy_send.at[jump, step], cy_recv.at[jump, step], (other, op)
+                spot, spot, cy_send.at[jump, step], cy_recv.at[jump, step], (target_sec, op)
             )
             copy.start()
             sends.append(copy)
@@ -416,6 +444,7 @@
         pltpu.SMEM(rdims.shape, jnp.int32),
         pltpu.VMEM((3, n_op, 8, 128), F32),
         pltpu.VMEM((3, n_sec, 8, 128), F32),
+        pltpu.VMEM((n_sec, n_op, 8, 128), F32), dma((n_sec, n_op)), dma((n_sec, n_op)),
         dma((10,)), dma,
         dma((n_chip, count_s)), dma((n_chip, count_s)),
         dma((n_chip, count_s)), dma((n_chip, count_s)),
@@ -443,7 +472,7 @@
         out_specs=(hbm, vmem, smem),
         scratch_shapes=scratch,
         compiler_params=pltpu.CompilerParams(
-            collective_id=0, has_side_effects=True, vmem_limit_bytes=40 * 1024 * 1024
+            collective_id=0, has_side_effects=True, vmem_limit_bytes=VMEM_BYTES
         ),
         cost_estimate=pl.CostEstimate(
             flops=2 * slots * 6 * block * block * width,

time: 79.3 us -> 74.4 us (0.938)
  local copies, waits for them, and re-layouts: 10.5 us -> 4.26 us
  Pallas kernels: 67.2 us -> 68.6 us
    unnamed x21 -> x3, local copies, waits for them, and re-layouts: 10.5 us -> 4.26 us
    pallas_call x1, Pallas kernels: 67.2 us -> 68.6 us  [on_device(): pl.pallas_call(body, name='davidson_step', out_shape=(jax.ShapeDtypeStruc...]
where the time goes in v3:
time: 74.4 us; the launch traced here: 74.2 us
  Pallas kernels  68.6 us (92%)
  local copies, waits for them, and re-layouts  4.26 us (6%)
  between operations  1.29 us (2%)
    pallas_call x1, Pallas kernels, on_device(): pl.pallas_call(body, name='davidson_step', out_shape=(jax.ShapeDtypeStruc...  68.6 us
    unnamed x3, local copies, waits for them, and re-layouts  4.26 us

profile of v3, /device:TPU:0, one launch (start us, length us, event | category | flops | bytes accessed | tf_op | source)
XLA Modules:
  0.0 74.2 jit_solution(817765944906661500)
XLA Ops:
  1.3 68.6 %davidson_step.1 = (bf16[2,256,256]{2,1,0:T(8,128)(2,1)}, f32[2,32,256]{2,1,0:T(8,128)}, f32[3]{0:T(128)}) custom-call(bf16[2,256,256]{2,1,0:T(8,128)(2,1)} %refs_0_.1, bf16[2,256,256]{2,1,0:T(8,128)(2,1)} %refs_1_.1, bf16[2,256,256]{2,1,0:T(8,128)(2,1)} %refs_2_.1, bf16[16,256,256]{2,1,0:T(8,128)(2,1)} %refs_3_.1, bf16[16,256,256]{2,1,0:T(8,128)(2,1)} %refs_4_.1, ...), custom_call_target="tpu_custom_call" | custom-call | flops 3221225472 | bytes 4194304 | tf_op jit(solution)/shard_map/davidson_step/pallas_call | solution.py:463
  69.9 1.7 %copy.17 = bf16[2,256,256]{2,1,0:T(8,128)(2,1)} copy(bf16[2,256,256]{2,1,0:T(8,128)(2,1)} %get-tuple-element.6) | data formatting | bytes 524288
  71.6 1.5 %copy.18 = f32[2,32,256]{2,1,0:T(8,128)} copy(f32[2,32,256]{2,1,0:T(8,128)} %get-tuple-element.7) | data formatting | bytes 131072
  73.0 1.1 %copy.19 = f32[3]{0:T(128)} copy(f32[3]{0:T(128)} %get-tuple-element.8) | data formatting | bytes 24
